TPU v7x, 32 devices: a whole 2x2x4 slice. The times are simulated.
32 devices in a mesh: band: 4 (over y, x), strip: 8 (over z, core).
Axes of the slice: x: 2, y: 2, z: 4, core: 2. Of those that a mesh axis runs over, the one named last changes fastest.
Arguments:
- cloud_field: bfloat16 [256, 256, 512], P('band', 'strip'), may hold values from -6 to 6
- row_gain: float32 [512], replicated, may hold values from 0.1 to 1.9
- row_qkv: bfloat16 [512, 1536], replicated, may hold values from -0.25 to 0.25
- row_out: bfloat16 [512, 512], replicated, may hold values from -1 to 1
- col_gain: float32 [512], replicated, may hold values from 0.1 to 1.9
- col_qkv: bfloat16 [512, 1536], replicated, may hold values from -0.25 to 0.25
- col_out: bfloat16 [512, 512], replicated, may hold values from -1 to 1
- plant_cell: int32 [4096], P(('band', 'strip')), may hold values from 0 to 2047
- plant_decoder_device: int32 [4096, 1], P(('band', 'strip')), may hold values from 0 to 31; in each aligned block of 128 rows (0 to 127, 128 to 255, ...) at most 8 rows name the same one
- plant_capacity: int32 [4096], P(('band', 'strip')), may hold values from 100 to 5000
- decode_first: bfloat16 [16384, 512], P(('band', 'strip')), may hold values from -0.25 to 0.25
- decode_second: bfloat16 [32, 512], P(('band', 'strip')), may hold values from -0.25 to 0.25
Outputs:
- final_field: bfloat16 [256, 256, 512], P('band', 'strip')
- plant_power: float32 [4096], P(('band', 'strip'))
- fleet_yield: float32 [], replicated
Inputs may be any that keep to these rules, and one draw needn't show every extreme that they name: `plant_decoder_device`: among the 128 plants listed on one device, no owner is named more than 8 times.
All inputs are finite; a program needn't handle non-finite values.
Results may differ from a plain program's by a relative error of at most 0.015.
Values may be sent and summed in bfloat16 or wider, within the bound.
A program may use at most 64 MiB of HBM per device.

v0:
```python
import jax
import jax.numpy as jnp
from jax import lax
from jax.experimental import pallas as pl
from jax.experimental.pallas import tpu as pltpu
from jax.sharding import PartitionSpec as P

HEADS = 8


EPS = 1e-06
TAU = 12.0


def norm_rows(values, scale_factor):
    widened = values.astype(jnp.float32)
    return (
        widened
        * lax.rsqrt(jnp.mean(widened * widened, axis=-1, keepdims=True) + EPS)
        * scale_factor
    )


def heads_norm(values):
    leading = values.shape[:-1]
    split_up = values.reshape(leading + (HEADS, values.shape[-1] // HEADS))
    normed = split_up * lax.rsqrt(jnp.mean(split_up * split_up, axis=-1, keepdims=True) + EPS)
    return normed.reshape(values.shape)


def project(tokens_in, scale_factor, weight_qkv):
    leading = tokens_in.shape[:-1]
    model_width = tokens_in.shape[-1]
    head_width = model_width // HEADS
    normed = norm_rows(tokens_in, scale_factor).astype(jnp.bfloat16).reshape(-1, model_width)
    projected = jnp.dot(normed, weight_qkv, preferred_element_type=jnp.float32)
    query = heads_norm(projected[:, :model_width]) * (TAU / head_width)
    keys_part = heads_norm(projected[:, model_width : 2 * model_width])
    values_part = projected[:, 2 * model_width :]
    shaped = leading + (model_width,)
    return (
        query.astype(jnp.bfloat16).reshape(shaped),
        keys_part.astype(jnp.bfloat16).reshape(shaped),
        values_part.astype(jnp.bfloat16).reshape(shaped),
    )


def attend(query, keys_part, values_part):
    batch_size, length, model_width = query.shape
    head_width = model_width // HEADS

    def split_heads(tensor):
        return tensor.reshape(batch_size, length, HEADS, head_width).transpose(2, 0, 1, 3)

    def one_head(operands):
        query_rows, key_rows, value_rows = operands
        attention_scores = jnp.einsum(
            "zxe,zle->zxl", query_rows, key_rows, preferred_element_type=jnp.float32
        )
        weights = jnp.exp(attention_scores)
        row_total = jnp.sum(weights, axis=-1, keepdims=True)
        weights_bfloat = (weights / row_total).astype(jnp.bfloat16)
        return jnp.einsum(
            "pem,pmj->pej", weights_bfloat, value_rows, preferred_element_type=jnp.float32
        ).astype(jnp.bfloat16)

    context = lax.map(
        one_head, (split_heads(query), split_heads(keys_part), split_heads(values_part))
    )
    return context.transpose(1, 2, 0, 3).reshape(batch_size, length, model_width)


def finish(tokens_in, context, weight_out):
    model_width = tokens_in.shape[-1]
    mixed = jnp.dot(
        context.reshape(-1, model_width), weight_out, preferred_element_type=jnp.float32
    )
    return (tokens_in.astype(jnp.float32) + mixed.reshape(tokens_in.shape)).astype(jnp.bfloat16)


def mix_layer(tokens_in, scale_factor, weight_qkv, weight_out):
    query, keys_part, values_part = project(tokens_in, scale_factor, weight_qkv)
    return finish(tokens_in, attend(query, keys_part, values_part), weight_out)


def sequence_layer(x, gain, weight_qkv, weight_out, head_sum):
    length, width = x.shape
    head = width // HEADS
    pair = 2 * head
    scale = lax.rsqrt(jnp.mean(x * x, axis=-1, keepdims=True) + EPS)
    normed = (x * scale * gain).astype(jnp.bfloat16)
    lane = lax.broadcasted_iota(jnp.int32, (length, pair), 1)
    even = lane < head
    half = head_sum.shape[0]

    def head_scale(part):
        squares = (part * part).astype(jnp.bfloat16)
        sums = jnp.dot(squares, head_sum, preferred_element_type=jnp.float32)
        return part * lax.rsqrt(sums * (1.0 / head) + EPS)

    ones_e = jnp.where(even, 1.0, 0.0).astype(jnp.bfloat16)
    ones_o = jnp.where(even, 0.0, 1.0).astype(jnp.bfloat16)
    zero = jnp.zeros((length, pair), jnp.float32)
    contexts = []
    for start in range(0, width, half):
        wide = slice(start, start + half)
        query = jnp.dot(normed, weight_qkv[:, wide], preferred_element_type=jnp.float32)
        keys = jnp.dot(
            normed,
            weight_qkv[:, width + start : width + start + half],
            preferred_element_type=jnp.float32,
        )
        values = jnp.dot(
            normed,
            weight_qkv[:, 2 * width + start : 2 * width + start + half],
            preferred_element_type=jnp.float32,
        )
        query = (head_scale(query) * (TAU / head)).astype(jnp.bfloat16)
        keys = head_scale(keys)
        for at in range(0, half, pair):
            k = keys[:, at : at + pair]
            v = values[:, at : at + pair]
            k_two = jnp.concatenate(
                [jnp.where(even, k, zero), jnp.where(even, zero, k)], axis=0
            ).astype(jnp.bfloat16)
            scores = lax.dot_general(
                query[:, at : at + pair],
                k_two,
                (((1,), (1,)), ((), ())),
                preferred_element_type=jnp.float32,
            )
            weights = jnp.exp(scores).astype(jnp.bfloat16)
            v_two = jnp.concatenate(
                [
                    jnp.concatenate([jnp.where(even, v, zero).astype(jnp.bfloat16), ones_e], axis=1),
                    jnp.concatenate([jnp.where(even, zero, v).astype(jnp.bfloat16), ones_o], axis=1),
                ],
                axis=0,
            )
            mixed = jnp.dot(weights, v_two, preferred_element_type=jnp.float32)
            contexts.append((mixed[:, :pair] / mixed[:, pair:]).astype(jnp.bfloat16))
    context = jnp.concatenate(contexts, axis=1)
    return x + jnp.dot(context, weight_out[...], preferred_element_type=jnp.float32)


def head_sum_matrix(width):
    head = width // HEADS
    index = jnp.arange(4 * head, dtype=jnp.int32) // head
    return (index[:, None] == index[None, :]).astype(jnp.bfloat16)


MESH = pl.DeviceIdType.MESH

def whole_kernel(
    cloud, row_gain, row_qkv, row_out, col_gain, col_qkv, col_out, head_sum,
    cells, place, capacity, first, second,
    final, returned,
    rows_in, mixed, rows_out, cols_in, columns, cols_out, blocks_in, field,
    sites_out, sites_in, yields_out,
    rows_sent, rows_got, turn_sent, turn_got, cols_sent, cols_got, site_sems,
):
    strips = lax.axis_size("strip")
    bands = lax.axis_size("band")
    devices = strips * bands
    strip = lax.axis_index("strip")
    band = lax.axis_index("band")
    me = band * strips + strip
    width = cloud.shape[2]
    length = columns.shape[0] // 4

    def wait_bytes(ref, sem):
        pltpu.make_async_copy(ref, ref, sem).wait()

    def split(number):
        return (number // strips, number % strips)

    barrier = pltpu.get_barrier_semaphore()

    @pl.loop(1, devices)
    def _(step):
        pl.semaphore_signal(
            barrier, inc=1, device_id=split((me + step) % devices), device_id_type=MESH
        )

    pl.semaphore_wait(barrier, devices - 1)

    @pl.loop(0, 2)
    def _(part):
        @pl.loop(1, strips)
        def _(step):
            to = (strip + step) % strips
            pltpu.make_async_remote_copy(
                src_ref=cloud.at[pl.ds(to * 8 + part * 4, 4)],
                dst_ref=rows_in.at[part, strip],
                send_sem=rows_sent.at[part],
                recv_sem=rows_got.at[part],
                device_id=(band, to),
                device_id_type=MESH,
            ).start()

        pltpu.make_async_copy(
            cloud.at[pl.ds(strip * 8 + part * 4, 4)], rows_in.at[part, strip], rows_got.at[part]
        ).start()

    @pl.loop(0, 2)
    def _(part):
        wait_bytes(rows_in.at[part], rows_got.at[part])

        @pl.loop(0, 4)
        def _(row):
            x = rows_in[part, :, row].astype(jnp.float32).reshape(length, width)
            y = sequence_layer(x, row_gain[...], row_qkv, row_out, head_sum[...])
            for lanes in range(0, width, 128):
                mixed[lanes // 128, :, pl.ds(pl.multiple_of(row * 8, 8), 8), :] = y[
                    :, lanes : lanes + 128
                ].reshape(devices, 8, 128)

        for parity in range(2):
            for lanes in range(0, width, 128):
                taken = mixed.at[lanes // 128].reshape(devices * 32, 128)[
                    pl.ds(parity, devices * 16, stride=2), :
                ]
                rows_out[part, parity, :, :, lanes : lanes + 128] = (
                    taken.astype(jnp.bfloat16).reshape(devices, 16, 128)
                )

            @pl.loop(1, devices)
            def _(step):
                to_band, to_strip = split((me + step) % devices)
                pltpu.make_async_remote_copy(
                    src_ref=rows_out.at[part, parity, to_strip * bands + to_band],
                    dst_ref=cols_in.at[parity, part, me],
                    send_sem=turn_sent.at[parity, part],
                    recv_sem=turn_got.at[parity, part],
                    device_id=(to_band, to_strip),
                    device_id_type=MESH,
                ).start()

            pltpu.make_async_copy(
                rows_out.at[part, parity, strip * bands + band],
                cols_in.at[parity, part, me],
                turn_got.at[parity, part],
            ).start()

    @pl.loop(0, 2)
    def _(parity):
        for part in range(2):
            wait_bytes(cols_in.at[parity, part], turn_got.at[parity, part])

            @pl.loop(0, devices)
            def _(src):
                at = pl.multiple_of(src * 32 + part * 16, 16)
                for lanes in range(0, width, 128):
                    columns[pl.ds(at, 16), lanes // 128, :] = cols_in[
                        parity, part, src, :, lanes : lanes + 128
                    ].astype(jnp.float32)

        @pl.loop(0, 4)
        def _(number):
            x = jnp.concatenate(
                [
                    columns[pl.ds(number, length, stride=4), lanes, :]
                    for lanes in range(width // 128)
                ],
                axis=1,
            )
            y = sequence_layer(x, col_gain[...], col_qkv, col_out, head_sum[...])
            col = parity * 4 + number
            cols_out[col] = y.astype(jnp.bfloat16).reshape(bands, length // bands, width)

            @pl.loop(1, bands)
            def _(step):
                to = (band + step) % bands
                pltpu.make_async_remote_copy(
                    src_ref=cols_out.at[col, to],
                    dst_ref=blocks_in.at[col, band],
                    send_sem=cols_sent.at[col],
                    recv_sem=cols_got.at[col],
                    device_id=(to, strip),
                    device_id_type=MESH,
                ).start()

            pltpu.make_async_copy(
                cols_out.at[col, band], blocks_in.at[col, band], cols_got.at[col]
            ).start()

    rows_here = cloud.shape[0]
    cols_here = cloud.shape[1]

    @pl.loop(0, 8)
    def _(col):
        wait_bytes(blocks_in.at[col], cols_got.at[col])
        for src in range(4):
            at = src * 8 + 2 * (col % 4) + col // 4
            for lanes in range(0, width, 128):
                field[lanes // 128, pl.ds(at, rows_here, stride=cols_here), :] = blocks_in[
                    col, src, :, lanes : lanes + 128
                ].astype(jnp.float32)

    @pl.loop(0, rows_here // 8)
    def _(row):
        tokens = pl.ds(pl.multiple_of(row * 8 * cols_here, 256), 8 * cols_here)
        for lanes in range(0, width, 128):
            final[pl.ds(row * 8, 8), :, lanes : lanes + 128] = (
                field[lanes // 128, tokens, :].astype(jnp.bfloat16).reshape(8, cols_here, 128)
            )

    tokens = rows_here * cols_here
    at_cell = (
        cells[...] == lax.broadcasted_iota(jnp.int32, (cells.shape[0], tokens), 1)
    ).astype(jnp.bfloat16)
    for lanes in range(0, width, 128):
        features = jnp.dot(
            at_cell, field[lanes // 128].astype(jnp.bfloat16), preferred_element_type=jnp.float32
        ).astype(jnp.bfloat16)
        slots = jnp.dot(place[...], features, preferred_element_type=jnp.float32)
        if lanes == 0:
            slots = slots + capacity[...]
        sites_out[:, :, lanes : lanes + 128] = slots.astype(jnp.bfloat16).reshape(devices, 16, 128)

    @pl.loop(1, devices)
    def _(step):
        to = (me + step) % devices
        pltpu.make_async_remote_copy(
            src_ref=sites_out.at[to],
            dst_ref=sites_in.at[me],
            send_sem=site_sems.at[0],
            recv_sem=site_sems.at[1],
            device_id=split(to),
            device_id_type=MESH,
        ).start()

    pltpu.make_async_copy(sites_out.at[me], sites_in.at[me], site_sems.at[1]).start()
    wait_bytes(sites_in, site_sems.at[1])

    arrived = sites_in[...].reshape(devices * 16, width)
    hidden = jax.nn.gelu(
        jnp.dot(arrived, first[...], preferred_element_type=jnp.float32)
    ).astype(jnp.bfloat16)
    logit = jnp.sum(
        hidden.astype(jnp.float32) * second[...].astype(jnp.float32), axis=1, keepdims=True
    )
    powers = jnp.maximum(logit, 0.0) + jnp.log1p(jnp.exp(-jnp.abs(logit)))
    powers = jnp.broadcast_to(powers, (devices * 16, 128)).reshape(devices, 16, 128)[:, :8]
    lane = lax.broadcasted_iota(jnp.int32, (devices, 8, 128), 2)
    digits = sites_in[:, :, :128].astype(jnp.float32)[:, 8:]
    weight = jnp.where(lane == 0, 0.128, jnp.where(lane == 1, 0.001, 0.0))
    total = jnp.sum(jnp.sum(digits * weight * powers, axis=2, keepdims=True), axis=(0, 1))
    yields_out[...] = jnp.where(lane < 64, powers, total[None, None, :])

    @pl.loop(1, devices)
    def _(step):
        to = (me + step) % devices
        pltpu.make_async_remote_copy(
            src_ref=yields_out.at[to],
            dst_ref=returned.at[me],
            send_sem=site_sems.at[2],
            recv_sem=site_sems.at[3],
            device_id=split(to),
            device_id_type=MESH,
        ).start()

    pltpu.make_async_copy(yields_out.at[me], returned.at[me], site_sems.at[3]).start()
    wait_bytes(returned, site_sems.at[3])

    for part in range(2):
        wait_bytes(rows_in.at[part, pl.ds(0, strips - 1)], rows_sent.at[part])
        for parity in range(2):
            wait_bytes(
                cols_in.at[parity, part, pl.ds(0, devices - 1)], turn_sent.at[parity, part]
            )
    for col in range(8):
        wait_bytes(cols_out.at[col, pl.ds(0, bands - 1)], cols_sent.at[col])
    wait_bytes(sites_out.at[pl.ds(0, devices - 1)], site_sems.at[0])
    wait_bytes(yields_out.at[pl.ds(0, devices - 1)], site_sems.at[2])


def fast_body(
    cloud_field,
    row_gain,
    row_qkv,
    row_out,
    col_gain,
    col_qkv,
    col_out,
    plant_cell,
    plant_decoder_device,
    plant_capacity,
    decode_first,
    decode_second,
):
    rows_here, cols_here, width = cloud_field.shape
    strips = lax.axis_size("strip")
    bands = lax.axis_size("band")
    devices = bands * strips
    length = cols_here * strips
    plants_here = plant_cell.shape[0]

    owners = plant_decoder_device[:, 0]
    counts = (owners[:, None] == jnp.arange(devices, dtype=jnp.int32)[None, :]).astype(jnp.int32)
    slot_of = jnp.sum(counts * (jnp.cumsum(counts, axis=0) - 1), axis=1)
    row_of = owners * 16 + slot_of
    numbers = jnp.arange(devices * 16, dtype=jnp.int32)[:, None]
    place = numbers == row_of[None, :]
    listed = jnp.sum(
        jnp.where(numbers == row_of[None, :] + 8, plant_capacity[None, :], 0),
        axis=1,
        keepdims=True,
    )
    lane = jnp.arange(128, dtype=jnp.int32)[None, :]
    capacity = jnp.where(
        lane == 0, listed // 128, jnp.where(lane == 1, listed % 128, 0)
    ).astype(jnp.float32)

    vmem = pl.BlockSpec(memory_space=pltpu.VMEM)
    bf16 = jnp.bfloat16
    final_field, returned = pl.pallas_call(
        whole_kernel,
        out_shape=(
            jax.ShapeDtypeStruct(cloud_field.shape, bf16),
            jax.ShapeDtypeStruct((devices, 8, 128), jnp.float32),
        ),
        in_specs=[pl.BlockSpec(memory_space=pl.ANY)] + [vmem] * 12,
        out_specs=(vmem, vmem),
        scratch_shapes=[
            pltpu.VMEM((2, strips, 4, cols_here, width), bf16),
            pltpu.VMEM((width // 128, devices, 32, 128), jnp.float32),
            pltpu.VMEM((2, 2, devices, 16, width), bf16),
            pltpu.VMEM((2, 2, devices, 16, width), bf16),
            pltpu.VMEM((4 * length, width // 128, 128), jnp.float32),
            pltpu.VMEM((8, bands, length // bands, width), bf16),
            pltpu.VMEM((8, bands, length // bands, width), bf16),
            pltpu.VMEM((width // 128, rows_here * cols_here, 128), jnp.float32),
            pltpu.VMEM((devices, 16, width), bf16),
            pltpu.VMEM((devices, 16, width), bf16),
            pltpu.VMEM((devices, 8, 128), jnp.float32),
            pltpu.SemaphoreType.DMA((2,)),
            pltpu.SemaphoreType.DMA((2,)),
            pltpu.SemaphoreType.DMA((2, 2)),
            pltpu.SemaphoreType.DMA((2, 2)),
            pltpu.SemaphoreType.DMA((8,)),
            pltpu.SemaphoreType.DMA((8,)),
            pltpu.SemaphoreType.DMA((4,)),
        ],
        compiler_params=pltpu.CompilerParams(
            collective_id=0, has_side_effects=True, vmem_limit_bytes=56 * 1024 * 1024
        ),
        cost_estimate=pl.CostEstimate(
            flops=4 * rows_here * cols_here * width * (4 * width + 2 * length),
            bytes_accessed=8 * cloud_field.size,
            transcendentals=2 * rows_here * cols_here * HEADS * length,
        ),
    )(
        cloud_field,
        row_gain.reshape(1, width),
        row_qkv,
        row_out,
        col_gain.reshape(1, width),
        col_qkv,
        col_out,
        head_sum_matrix(width),
        plant_cell[:, None],
        place.astype(bf16),
        capacity,
        decode_first,
        decode_second,
    )
    yields = jnp.pad(returned[:, :, 0], ((0, 0), (0, 8))).reshape(devices * 16, 1)
    own_yield = jnp.sum(jnp.where(place, yields, 0.0), axis=0)
    plant_power = plant_capacity.astype(jnp.float32) * 0.001 * own_yield
    fleet_yield = jnp.sum(returned[:, 0, 127]) / float(plants_here * devices)
    return (final_field, plant_power, fleet_yield)


def body(
    cloud_field,
    row_gain,
    row_qkv,
    row_out,
    col_gain,
    col_qkv,
    col_out,
    plant_cell,
    plant_decoder_device,
    plant_capacity,
    decode_first,
    decode_second,
):
    rows_here, cols_here, model_width = cloud_field.shape
    strips = lax.axis_size("strip")
    bands = lax.axis_size("band")
    owner_count = bands * strips
    row_share = rows_here // strips
    col_share = cols_here // bands
    shape_send = (strips, row_share, cols_here, model_width)
    mixed_rows = mix_layer(
        lax.all_to_all(
            cloud_field.reshape(shape_send), "strip", split_axis=0, concat_axis=2, tiled=True
        )[0],
        row_gain,
        row_qkv,
        row_out,
    )[None]
    after_rows = lax.all_to_all(
        mixed_rows, "strip", split_axis=2, concat_axis=0, tiled=True
    ).reshape(rows_here, cols_here, model_width)
    turned = lax.all_to_all(
        after_rows.reshape(rows_here, bands, col_share, model_width),
        "band",
        split_axis=1,
        concat_axis=0,
        tiled=True,
    )[:, 0].transpose(1, 0, 2)
    mixed_cols = mix_layer(turned, col_gain, col_qkv, col_out)
    columns_done = mixed_cols.transpose(1, 0, 2)[:, None]
    final_field = lax.all_to_all(
        columns_done, "band", split_axis=0, concat_axis=1, tiled=True
    ).reshape(rows_here, cols_here, model_width)
    plants_here = plant_cell.shape[0]
    most_slots = 2 * plants_here // owner_count
    flat_field = final_field.reshape(rows_here * cols_here, model_width)
    features = flat_field[plant_cell]
    owners = plant_decoder_device[:, 0]
    one_hot = (owners[:, None] == jnp.arange(owner_count, dtype=jnp.int32)[None, :]).astype(
        jnp.int32
    )
    running = jnp.cumsum(one_hot, axis=0)
    slot_of = jnp.sum(one_hot * (running - 1), axis=1)
    destination = owners * most_slots + slot_of
    send_buffer = (
        jnp.zeros((owner_count * most_slots, model_width), jnp.bfloat16)
        .at[destination]
        .set(features)
    )
    send_buffer = send_buffer.reshape(owner_count, most_slots, model_width)
    hidden = jax.nn.gelu(
        jnp.einsum(
            "smd,dh->smh",
            lax.all_to_all(send_buffer, ("band", "strip"), split_axis=0, concat_axis=0, tiled=True),
            decode_first,
            preferred_element_type=jnp.float32,
        )
    ).astype(jnp.bfloat16)
    output_logit = jnp.einsum(
        "smh,h->sm", hidden, decode_second[0], preferred_element_type=jnp.float32
    )
    yields = jax.nn.softplus(output_logit)
    returned = lax.all_to_all(yields, ("band", "strip"), split_axis=0, concat_axis=0, tiled=True)
    own_yield = returned.reshape(-1)[destination]
    capacity_w = plant_capacity.astype(jnp.float32) * 0.001
    plant_power = capacity_w * own_yield
    power_sum = lax.psum(jnp.sum(plant_power), ("band", "strip"))
    fleet_yield = power_sum / float(plants_here * owner_count)
    return (final_field, plant_power, fleet_yield)


def solution(mesh):
    grid_fits = 32 * mesh.shape["strip"] == 256 and 64 * mesh.shape["band"] == 256
    return jax.shard_map(
        fast_body if grid_fits else body,
        mesh=mesh,
        in_specs=(
            P("band", "strip", None),
            P(),
            P(),
            P(),
            P(),
            P(),
            P(),
            P(("band", "strip")),
            P(("band", "strip"), None),
            P(("band", "strip")),
            P(("band", "strip"), None),
            P(("band", "strip"), None),
        ),
        out_specs=(P("band", "strip", None), P(("band", "strip")), P()),
        check_vma=False,
    )
```

profile of v0, /device:TPU:0, one launch (start us, length us, event | category | flops | bytes accessed | tf_op | source)
XLA Modules:
  0.0 162.7 jit_solution(10130003745684741920)
XLA Ops:
  0.6 0.7 fusion.1
  1.4 0.2 reduce_window_sum.11
  1.5 0.8 select_reduce_fusion.2
  2.4 0.7 broadcast_add_fusion
  3.0 0.8 select_reduce_fusion.1
  3.9 0.9 select_convert_fusion.capacity
  4.8 0.7 fusion.place
  5.5 0.8 compare_convert_fusion.head_sum
  6.2 1.4 copy.16.cells
  7.6 0.0 copy-start
  7.6 146.6 %shard_map.139 = (bf16[64,32,512]{2,1,0:T(8,128)(2,1)}, f32[32,8,128]{2,1,0:T(8,128)}) custom-call(bf16[64,32,512]{2,1,0:T(8,128)(2,1)} %cloud.1, f32[1,512]{1,0:T(1,128)} %bitcast.14, bf16[512,1536]{1,0:T(8,128)(2,1)} %row_qkv.1, bf16[512,512]{1,0:T(8,128)(2,1)} %row_out.1, f32[1,512]{1,0:T(1,128)} %bitcast.15, bf16[512,1536]{1,0:T(8,128)(2,1)} %col_qkv.1, ...), custom_call_target="tpu_custom_call" | custom-call | flops 10737418240 | bytes 8388608 | tf_op jit(solution)/shard_map/pallas_call | solution.py:417
  154.2 1.1 copy.20
  155.4 0.1 broadcast_in_dim.79
  155.5 0.2 select_reduce_fusion
  155.6 0.0 copy-done
  155.7 0.5 multiply_multiply_fusion
  156.2 1.6 slice_reduce_fusion
  158.4 3.2 %copy.22 = bf16[64,32,512]{2,1,0:T(8,128)(2,1)} copy(bf16[64,32,512]{2,1,0:T(8,128)(2,1)} %get-tuple-element.16) | data formatting | bytes 4194304
  (4 shorter events, 0.0 us)
Async XLA Ops:
  7.6 148.0 %copy-start = (s32[128]{0:T(128)S(1)}, s32[128]{0:T(128)}, u32[]{:S(2)}) copy-start(s32[128]{0:T(128)} %param.21) | copy-start | bytes 1540
where the time goes:
time: 163 us
  Pallas kernels  147 us (90%)
  other arithmetic  7.86 us (5%)
  local copies, waits for them, and re-layouts  5.78 us (4%)
  between operations  2.47 us (2%)
    pallas_call x1, Pallas kernels, fast_body(): pl.pallas_call(whole_kernel, out_shape=(jax.ShapeDtypeStruct(cloud_field....  147 us

commit v1 on v0

--- a/solution.py
+++ b/solution.py
@@ -153,11 +153,11 @@
 
 def whole_kernel(
     cloud, row_gain, row_qkv, row_out, col_gain, col_qkv, col_out, head_sum,
-    cells, place, capacity, first, second,
-    final, returned,
-    rows_in, mixed, rows_out, cols_in, columns, cols_out, blocks_in, field,
-    sites_out, sites_in, yields_out,
-    rows_sent, rows_got, turn_sent, turn_got, cols_sent, cols_got, site_sems,
+    cells, owners, capacity, first, second,
+    final, power, fleet,
+    rows_in, mixed, rows_out, cols_in, columns, cols_out, blocks_in, picks,
+    sites_out, sites_in, listed_out, listed_in, yields_out, returned,
+    rows_sent, rows_got, turn_sent, turn_got, cols_sent, cols_got, site_sems, done_sems,
 ):
     strips = lax.axis_size("strip")
     bands = lax.axis_size("band")
@@ -202,6 +202,70 @@
             cloud.at[pl.ds(strip * 8 + part * 4, 4)], rows_in.at[part, strip], rows_got.at[part]
         ).start()
 
+    plants = cells.shape[1]
+    slots = 8
+    owner_hot = lax.broadcasted_iota(jnp.int32, (devices, plants), 0) == owners[...]
+    owner_one = jnp.where(owner_hot, 1.0, 0.0)
+    before = (
+        lax.broadcasted_iota(jnp.int32, (plants, plants), 0)
+        < lax.broadcasted_iota(jnp.int32, (plants, plants), 1)
+    )
+    earlier = jnp.dot(
+        owner_one.astype(jnp.bfloat16),
+        jnp.where(before, 1.0, 0.0).astype(jnp.bfloat16),
+        preferred_element_type=jnp.float32,
+    )
+    slot = jnp.sum(owner_one * earlier, axis=0, keepdims=True).astype(jnp.int32)
+    spot = owners[...] * slots + slot
+    place = jnp.where(
+        lax.broadcasted_iota(jnp.int32, (devices * slots, plants), 0) == spot, 1.0, 0.0
+    )
+    lane = lax.broadcasted_iota(jnp.int32, (devices, slots, 128), 2)
+    own_lane = lane == lax.broadcasted_iota(jnp.int32, (devices, slots, 128), 1)
+
+    def to_lanes(column):
+        wide = jnp.broadcast_to(column, (devices * slots, 128)).reshape(devices, slots, 128)
+        return jnp.sum(jnp.where(own_lane, wide, 0.0), axis=1, keepdims=True)
+
+    kilowatts = capacity[...].astype(jnp.float32)
+    listed_out[...] = to_lanes(jnp.sum(place * kilowatts, axis=1, keepdims=True))
+
+    @pl.loop(1, devices)
+    def _(step):
+        to = (me + step) % devices
+        pltpu.make_async_remote_copy(
+            src_ref=listed_out.at[to],
+            dst_ref=listed_in.at[me],
+            send_sem=site_sems.at[4],
+            recv_sem=site_sems.at[5],
+            device_id=split(to),
+            device_id_type=MESH,
+        ).start()
+
+    pltpu.make_async_copy(listed_out.at[me], listed_in.at[me], site_sems.at[5]).start()
+
+    rows_here = cloud.shape[0]
+    cols_here = cloud.shape[1]
+    cell_row = cells[...] // cols_here
+    cell_col = cells[...] % cols_here
+    in_block = cell_col // 8 * rows_here + cell_row
+    block = cell_col % 2 * 4 + cell_col % 8 // 2
+
+    @pl.loop(0, 8)
+    def _(col):
+        at_cell = jnp.where(
+            lax.broadcasted_iota(jnp.int32, (length, plants), 0)
+            == jnp.where(block == col, in_block, -1),
+            1.0,
+            0.0,
+        )
+        picks[col] = lax.dot_general(
+            place.astype(jnp.bfloat16),
+            at_cell.astype(jnp.bfloat16),
+            (((1,), (1,)), ((), ())),
+            preferred_element_type=jnp.float32,
+        ).astype(jnp.bfloat16)
+
     @pl.loop(0, 2)
     def _(part):
         wait_bytes(rows_in.at[part], rows_got.at[part])
@@ -284,39 +348,20 @@
                 cols_out.at[col, band], blocks_in.at[col, band], cols_got.at[col]
             ).start()
 
-    rows_here = cloud.shape[0]
-    cols_here = cloud.shape[1]
-
-    @pl.loop(0, 8)
-    def _(col):
+    sites = jnp.zeros((devices * slots, width), jnp.float32)
+    for col in range(8):
         wait_bytes(blocks_in.at[col], cols_got.at[col])
-        for src in range(4):
-            at = src * 8 + 2 * (col % 4) + col // 4
-            for lanes in range(0, width, 128):
-                field[lanes // 128, pl.ds(at, rows_here, stride=cols_here), :] = blocks_in[
-                    col, src, :, lanes : lanes + 128
-                ].astype(jnp.float32)
-
-    @pl.loop(0, rows_here // 8)
-    def _(row):
-        tokens = pl.ds(pl.multiple_of(row * 8 * cols_here, 256), 8 * cols_here)
-        for lanes in range(0, width, 128):
-            final[pl.ds(row * 8, 8), :, lanes : lanes + 128] = (
-                field[lanes // 128, tokens, :].astype(jnp.bfloat16).reshape(8, cols_here, 128)
-            )
-
-    tokens = rows_here * cols_here
-    at_cell = (
-        cells[...] == lax.broadcasted_iota(jnp.int32, (cells.shape[0], tokens), 1)
-    ).astype(jnp.bfloat16)
-    for lanes in range(0, width, 128):
-        features = jnp.dot(
-            at_cell, field[lanes // 128].astype(jnp.bfloat16), preferred_element_type=jnp.float32
-        ).astype(jnp.bfloat16)
-        slots = jnp.dot(place[...], features, preferred_element_type=jnp.float32)
-        if lanes == 0:
-            slots = slots + capacity[...]
-        sites_out[:, :, lanes : lanes + 128] = slots.astype(jnp.bfloat16).reshape(devices, 16, 128)
+        pltpu.make_async_copy(blocks_in.at[col], final.at[col], done_sems.at[col]).start()
+        sites = sites + jnp.dot(
+            picks[col],
+            blocks_in[col].reshape(length, width),
+            preferred_element_type=jnp.float32,
+        )
+    sites = sites.reshape(devices, slots, width)
+    half = width // 2
+    sites_out[...] = jnp.concatenate([sites[:, :, :half], sites[:, :, half:]], axis=1).astype(
+        jnp.bfloat16
+    )
 
     @pl.loop(1, devices)
     def _(step):
@@ -331,22 +376,24 @@
         ).start()
 
     pltpu.make_async_copy(sites_out.at[me], sites_in.at[me], site_sems.at[1]).start()
+    wait_bytes(listed_in, site_sems.at[5])
     wait_bytes(sites_in, site_sems.at[1])
 
-    arrived = sites_in[...].reshape(devices * 16, width)
-    hidden = jax.nn.gelu(
-        jnp.dot(arrived, first[...], preferred_element_type=jnp.float32)
-    ).astype(jnp.bfloat16)
-    logit = jnp.sum(
-        hidden.astype(jnp.float32) * second[...].astype(jnp.float32), axis=1, keepdims=True
-    )
-    powers = jnp.maximum(logit, 0.0) + jnp.log1p(jnp.exp(-jnp.abs(logit)))
-    powers = jnp.broadcast_to(powers, (devices * 16, 128)).reshape(devices, 16, 128)[:, :8]
-    lane = lax.broadcasted_iota(jnp.int32, (devices, 8, 128), 2)
-    digits = sites_in[:, :, :128].astype(jnp.float32)[:, 8:]
-    weight = jnp.where(lane == 0, 0.128, jnp.where(lane == 1, 0.001, 0.0))
-    total = jnp.sum(jnp.sum(digits * weight * powers, axis=2, keepdims=True), axis=(0, 1))
-    yields_out[...] = jnp.where(lane < 64, powers, total[None, None, :])
+    arrived = sites_in[...].astype(jnp.float32)
+    hidden = jnp.dot(
+        arrived[:, :slots].reshape(devices * slots, half).astype(jnp.bfloat16),
+        first[:half, :],
+        preferred_element_type=jnp.float32,
+    ) + jnp.dot(
+        arrived[:, slots:].reshape(devices * slots, half).astype(jnp.bfloat16),
+        first[half:, :],
+        preferred_element_type=jnp.float32,
+    )
+    hidden = jax.nn.gelu(hidden).astype(jnp.bfloat16).astype(jnp.float32)
+    logit = jnp.sum(hidden * second[...].astype(jnp.float32), axis=1, keepdims=True)
+    yields = to_lanes(jnp.maximum(logit, 0.0) + jnp.log1p(jnp.exp(-jnp.abs(logit))))
+    total = jnp.sum(yields * listed_in[...] * 0.001, axis=(0, 2), keepdims=True)
+    yields_out[...] = jnp.where(lane[:, :1] == slots, total, yields)
 
     @pl.loop(1, devices)
     def _(step):
@@ -361,7 +408,6 @@
         ).start()
 
     pltpu.make_async_copy(yields_out.at[me], returned.at[me], site_sems.at[3]).start()
-    wait_bytes(returned, site_sems.at[3])
 
     for part in range(2):
         wait_bytes(rows_in.at[part, pl.ds(0, strips - 1)], rows_sent.at[part])
@@ -371,7 +417,23 @@
             )
     for col in range(8):
         wait_bytes(cols_out.at[col, pl.ds(0, bands - 1)], cols_sent.at[col])
+        wait_bytes(blocks_in.at[col], done_sems.at[col])
     wait_bytes(sites_out.at[pl.ds(0, devices - 1)], site_sems.at[0])
+    wait_bytes(listed_out.at[pl.ds(0, devices - 1)], site_sems.at[4])
+
+    wait_bytes(returned, site_sems.at[3])
+    back = returned[...].reshape(devices, 128)
+    by_slot = lax.dot_general(
+        back,
+        owner_one,
+        (((0,), (0,)), ((), ())),
+        precision=lax.Precision.HIGHEST,
+        preferred_element_type=jnp.float32,
+    )
+    own = lax.broadcasted_iota(jnp.int32, (128, plants), 0) == slot
+    power[...] = kilowatts * 0.001 * jnp.sum(jnp.where(own, by_slot, 0.0), axis=0, keepdims=True)
+    sums = jnp.sum(jnp.where(lane[:, 0] == slots, back, 0.0), axis=(0, 1), keepdims=True)
+    fleet[...] = jnp.broadcast_to(sums / float(plants * devices), fleet.shape)
     wait_bytes(yields_out.at[pl.ds(0, devices - 1)], site_sems.at[2])
 
 
@@ -396,32 +458,17 @@
     length = cols_here * strips
     plants_here = plant_cell.shape[0]
 
-    owners = plant_decoder_device[:, 0]
-    counts = (owners[:, None] == jnp.arange(devices, dtype=jnp.int32)[None, :]).astype(jnp.int32)
-    slot_of = jnp.sum(counts * (jnp.cumsum(counts, axis=0) - 1), axis=1)
-    row_of = owners * 16 + slot_of
-    numbers = jnp.arange(devices * 16, dtype=jnp.int32)[:, None]
-    place = numbers == row_of[None, :]
-    listed = jnp.sum(
-        jnp.where(numbers == row_of[None, :] + 8, plant_capacity[None, :], 0),
-        axis=1,
-        keepdims=True,
-    )
-    lane = jnp.arange(128, dtype=jnp.int32)[None, :]
-    capacity = jnp.where(
-        lane == 0, listed // 128, jnp.where(lane == 1, listed % 128, 0)
-    ).astype(jnp.float32)
-
     vmem = pl.BlockSpec(memory_space=pltpu.VMEM)
     bf16 = jnp.bfloat16
-    final_field, returned = pl.pallas_call(
+    final, power, fleet = pl.pallas_call(
         whole_kernel,
         out_shape=(
-            jax.ShapeDtypeStruct(cloud_field.shape, bf16),
-            jax.ShapeDtypeStruct((devices, 8, 128), jnp.float32),
+            jax.ShapeDtypeStruct((8, bands, rows_here, width), bf16),
+            jax.ShapeDtypeStruct((1, plants_here), jnp.float32),
+            jax.ShapeDtypeStruct((1, 128), jnp.float32),
         ),
         in_specs=[pl.BlockSpec(memory_space=pl.ANY)] + [vmem] * 12,
-        out_specs=(vmem, vmem),
+        out_specs=(pl.BlockSpec(memory_space=pl.ANY), vmem, vmem),
         scratch_shapes=[
             pltpu.VMEM((2, strips, 4, cols_here, width), bf16),
             pltpu.VMEM((width // 128, devices, 32, 128), jnp.float32),
@@ -430,17 +477,21 @@
             pltpu.VMEM((4 * length, width // 128, 128), jnp.float32),
             pltpu.VMEM((8, bands, length // bands, width), bf16),
             pltpu.VMEM((8, bands, length // bands, width), bf16),
-            pltpu.VMEM((width // 128, rows_here * cols_here, 128), jnp.float32),
-            pltpu.VMEM((devices, 16, width), bf16),
-            pltpu.VMEM((devices, 16, width), bf16),
-            pltpu.VMEM((devices, 8, 128), jnp.float32),
+            pltpu.VMEM((8, devices * 8, length), bf16),
+            pltpu.VMEM((devices, 16, width // 2), bf16),
+            pltpu.VMEM((devices, 16, width // 2), bf16),
+            pltpu.VMEM((devices, 1, 128), jnp.float32),
+            pltpu.VMEM((devices, 1, 128), jnp.float32),
+            pltpu.VMEM((devices, 1, 128), jnp.float32),
+            pltpu.VMEM((devices, 1, 128), jnp.float32),
             pltpu.SemaphoreType.DMA((2,)),
             pltpu.SemaphoreType.DMA((2,)),
             pltpu.SemaphoreType.DMA((2, 2)),
             pltpu.SemaphoreType.DMA((2, 2)),
             pltpu.SemaphoreType.DMA((8,)),
             pltpu.SemaphoreType.DMA((8,)),
-            pltpu.SemaphoreType.DMA((4,)),
+            pltpu.SemaphoreType.DMA((6,)),
+            pltpu.SemaphoreType.DMA((8,)),
         ],
         compiler_params=pltpu.CompilerParams(
             collective_id=0, has_side_effects=True, vmem_limit_bytes=56 * 1024 * 1024
@@ -459,17 +510,18 @@
         col_qkv,
         col_out,
         head_sum_matrix(width),
-        plant_cell[:, None],
-        place.astype(bf16),
-        capacity,
+        plant_cell.reshape(1, plants_here),
+        plant_decoder_device.reshape(1, plants_here),
+        plant_capacity.reshape(1, plants_here),
         decode_first,
         decode_second,
     )
-    yields = jnp.pad(returned[:, :, 0], ((0, 0), (0, 8))).reshape(devices * 16, 1)
-    own_yield = jnp.sum(jnp.where(place, yields, 0.0), axis=0)
-    plant_power = plant_capacity.astype(jnp.float32) * 0.001 * own_yield
-    fleet_yield = jnp.sum(returned[:, 0, 127]) / float(plants_here * devices)
-    return (final_field, plant_power, fleet_yield)
+    final_field = (
+        final.reshape(2, 4, bands, rows_here, width)
+        .transpose(3, 2, 1, 0, 4)
+        .reshape(rows_here, cols_here, width)
+    )
+    return (final_field, power[0], fleet[0, 0])
 
 
 def body(

time: 163 us -> 147 us (0.902)
  Pallas kernels: 147 us -> 138 us
  other arithmetic: 7.86 us -> 0.76 us
    pallas_call x1, Pallas kernels: 147 us -> 138 us  [fast_body(): pl.pallas_call(whole_kernel, out_shape=(jax.ShapeDtypeStruct((8, bands, r...]
    transpose x0 -> x1, local copies, waits for them, and re-layouts: none -> 3.75 us  [fast_body(): final_field = final.reshape(2, 4, bands, rows_here, width).transpose(3, 2...]
    reduce_sum x4 -> x0, other arithmetic: 3.4 us -> none  [the longest x1 1.61 us: fast_body(): fleet_yield = jnp.sum(returned[:, 0, 127]) / float(plants_here * devices)]
    unnamed x3 -> x5, local copies, waits for them, and re-layouts: 3.16 us -> 0.52 us
    convert_element_type x3 -> x0, other arithmetic: 2.33 us -> none  [the longest x1 0.91 us: fast_body(): capacity = jnp.where(lane == 0, listed // 128, jnp.where(lane == 1, liste...]
    reshape x0 -> x1, local copies, waits for them, and re-layouts: none -> 2.21 us  [fast_body(): final_field = final.reshape(2, 4, bands, rows_here, width).transpose(3, 2...]
where the time goes in v1:
time: 147 us
  Pallas kernels  138 us (94%)
  local copies, waits for them, and re-layouts  6.48 us (4%)
  between operations  1.83 us (1%)
    pallas_call x1, Pallas kernels, fast_body(): pl.pallas_call(whole_kernel, out_shape=(jax.ShapeDtypeStruct((8, bands, r...  138 us
    transpose x1, local copies, waits for them, and re-layouts, fast_body(): final_field = final.reshape(2, 4, bands, rows_here, width).transpose(3, 2...  3.75 us

profile of v1, /device:TPU:0, one launch (start us, length us, event | category | flops | bytes accessed | tf_op | source)
XLA Modules:
  0.0 147.0 jit_solution(5107714395316586434)
XLA Ops:
  0.6 0.8 compare_convert_fusion.head_sum
  1.4 137.9 %shard_map.139 = (bf16[8,4,64,512]{3,2,1,0:T(8,128)(2,1)}, f32[1,128]{1,0:T(1,128)}, f32[1,128]{1,0:T(1,128)}) custom-call(bf16[64,32,512]{2,1,0:T(8,128)(2,1)} %cloud.1, f32[1,512]{1,0:T(1,128)} %bitcast.12, bf16[512,1536]{1,0:T(8,128)(2,1)} %row_qkv.1, bf16[512,512]{1,0:T(8,128)(2,1)} %row_out.1, f32[1,512]{1,0:T(1,128)} %bitcast.13, ...), custom_call_target="tpu_custom_call" | custom-call | flops 10737418240 | bytes 8388608 | tf_op jit(solution)/shard_map/pallas_call | solution.py:463
  139.4 3.7 %copy.15 = bf16[64,4,4,2,512]{4,3,2,1,0:T(2,128)(2,1)S(1)} copy(bf16[64,4,4,2,512]{4,0,1,2,3:T(8,128)(2,1)} %bitcast.11) | data formatting | bytes 4194304 | tf_op jit(solution)/shard_map/transpose | solution.py:521
  143.1 0.0 copy-start.1
  143.1 0.0 copy-start
  143.1 2.2 %reshape.59 = bf16[64,32,512]{2,1,0:T(8,128)(2,1)} reshape(bf16[64,4,4,2,512]{4,3,2,1,0:T(2,128)(2,1)S(1)} %copy.15) | data formatting | bytes 4194304 | tf_op jit(solution)/shard_map/reshape | solution.py:522
  145.3 0.0 copy-done.1
  145.3 0.5 copy.18
  145.8 0.0 copy-done
  (1 shorter events, 0.0 us)
Async XLA Ops:
  143.1 2.2 %copy-start.1 = (f32[1,128]{1,0:T(1,128)S(1)}, f32[1,128]{1,0:T(1,128)}, u32[]{:S(2)}) copy-start(f32[1,128]{1,0:T(1,128)} %get-tuple-element.7) | copy-start | bytes 1540
  143.1 2.7 %copy-start = (f32[1,128]{1,0:T(1,128)S(1)}, f32[1,128]{1,0:T(1,128)}, u32[]{:S(2)}) copy-start(f32[1,128]{1,0:T(1,128)} %get-tuple-element.8) | copy-start | bytes 1540

commit v2 on v1

--- a/solution.py
+++ b/solution.py
@@ -10,6 +10,7 @@
 
 EPS = 1e-06
 TAU = 12.0
+LOG2_E = 1.4426950408889634
 
 
 def norm_rows(values, scale_factor):
@@ -115,7 +116,7 @@
             weight_qkv[:, 2 * width + start : 2 * width + start + half],
             preferred_element_type=jnp.float32,
         )
-        query = (head_scale(query) * (TAU / head)).astype(jnp.bfloat16)
+        query = (head_scale(query) * (TAU / head * LOG2_E)).astype(jnp.bfloat16)
         keys = head_scale(keys)
         for at in range(0, half, pair):
             k = keys[:, at : at + pair]
@@ -129,7 +130,7 @@
                 (((1,), (1,)), ((), ())),
                 preferred_element_type=jnp.float32,
             )
-            weights = jnp.exp(scores).astype(jnp.bfloat16)
+            weights = jnp.exp2(scores).astype(jnp.bfloat16)
             v_two = jnp.concatenate(
                 [
                     jnp.concatenate([jnp.where(even, v, zero).astype(jnp.bfloat16), ones_e], axis=1),
@@ -166,7 +167,7 @@
     band = lax.axis_index("band")
     me = band * strips + strip
     width = cloud.shape[2]
-    length = columns.shape[0] // 4
+    length = columns.shape[1] // 4
 
     def wait_bytes(ref, sem):
         pltpu.make_async_copy(ref, ref, sem).wait()
@@ -184,13 +185,13 @@
 
     pl.semaphore_wait(barrier, devices - 1)
 
-    @pl.loop(0, 2)
+    @pl.loop(0, 4)
     def _(part):
         @pl.loop(1, strips)
         def _(step):
             to = (strip + step) % strips
             pltpu.make_async_remote_copy(
-                src_ref=cloud.at[pl.ds(to * 8 + part * 4, 4)],
+                src_ref=cloud.at[pl.ds(to * 8 + part * 2, 2)],
                 dst_ref=rows_in.at[part, strip],
                 send_sem=rows_sent.at[part],
                 recv_sem=rows_got.at[part],
@@ -199,7 +200,7 @@
             ).start()
 
         pltpu.make_async_copy(
-            cloud.at[pl.ds(strip * 8 + part * 4, 4)], rows_in.at[part, strip], rows_got.at[part]
+            cloud.at[pl.ds(strip * 8 + part * 2, 2)], rows_in.at[part, strip], rows_got.at[part]
         ).start()
 
     plants = cells.shape[1]
@@ -268,11 +269,15 @@
 
     @pl.loop(0, 2)
     def _(part):
-        wait_bytes(rows_in.at[part], rows_got.at[part])
-
         @pl.loop(0, 4)
         def _(row):
-            x = rows_in[part, :, row].astype(jnp.float32).reshape(length, width)
+            pair = part * 2 + row // 2
+
+            @pl.when(row % 2 == 0)
+            def _():
+                wait_bytes(rows_in.at[pair], rows_got.at[pair])
+
+            x = rows_in[pair, :, row % 2].astype(jnp.float32).reshape(length, width)
             y = sequence_layer(x, row_gain[...], row_qkv, row_out, head_sum[...])
             for lanes in range(0, width, 128):
                 mixed[lanes // 128, :, pl.ds(pl.multiple_of(row * 8, 8), 8), :] = y[
@@ -315,7 +320,7 @@
             def _(src):
                 at = pl.multiple_of(src * 32 + part * 16, 16)
                 for lanes in range(0, width, 128):
-                    columns[pl.ds(at, 16), lanes // 128, :] = cols_in[
+                    columns[lanes // 128, pl.ds(at, 16), :] = cols_in[
                         parity, part, src, :, lanes : lanes + 128
                     ].astype(jnp.float32)
 
@@ -323,7 +328,7 @@
         def _(number):
             x = jnp.concatenate(
                 [
-                    columns[pl.ds(number, length, stride=4), lanes, :]
+                    columns[lanes, pl.ds(number, length, stride=4), :]
                     for lanes in range(width // 128)
                 ],
                 axis=1,
@@ -409,8 +414,9 @@
 
     pltpu.make_async_copy(yields_out.at[me], returned.at[me], site_sems.at[3]).start()
 
+    for pair in range(4):
+        wait_bytes(rows_in.at[pair, pl.ds(0, strips - 1)], rows_sent.at[pair])
     for part in range(2):
-        wait_bytes(rows_in.at[part, pl.ds(0, strips - 1)], rows_sent.at[part])
         for parity in range(2):
             wait_bytes(
                 cols_in.at[parity, part, pl.ds(0, devices - 1)], turn_sent.at[parity, part]
@@ -435,6 +441,39 @@
     sums = jnp.sum(jnp.where(lane[:, 0] == slots, back, 0.0), axis=(0, 1), keepdims=True)
     fleet[...] = jnp.broadcast_to(sums / float(plants * devices), fleet.shape)
     wait_bytes(yields_out.at[pl.ds(0, devices - 1)], site_sems.at[2])
+
+
+def assemble_kernel(blocks, out, tile):
+    parts, bands, rows, width = blocks.shape
+    cols = parts * bands
+    for lanes in range(0, width, 128):
+        for part in range(parts):
+            for band in range(bands):
+                at = band * parts + 2 * (part % 4) + part // 4
+                tile[lanes // 128, pl.ds(at, rows, stride=cols), :] = blocks[
+                    part, band, :, lanes : lanes + 128
+                ].astype(jnp.float32)
+        out[:, :, lanes : lanes + 128] = (
+            tile[lanes // 128].astype(jnp.bfloat16).reshape(rows, cols, 128)
+        )
+
+
+def assemble(blocks):
+    parts, bands, rows, width = blocks.shape
+    step = 16
+    cols = parts * bands
+    return pl.pallas_call(
+        assemble_kernel,
+        grid=(rows // step,),
+        out_shape=jax.ShapeDtypeStruct((rows, cols, width), blocks.dtype),
+        in_specs=[pl.BlockSpec((parts, bands, step, width), lambda i: (0, 0, i, 0))],
+        out_specs=pl.BlockSpec((step, cols, width), lambda i: (i, 0, 0)),
+        scratch_shapes=[pltpu.VMEM((width // 128, step * cols, 128), jnp.float32)],
+        compiler_params=pltpu.CompilerParams(vmem_limit_bytes=60 * 1024 * 1024),
+        cost_estimate=pl.CostEstimate(
+            flops=0, bytes_accessed=4 * blocks.size, transcendentals=0
+        ),
+    )(blocks)
 
 
 def fast_body(
@@ -470,11 +509,11 @@
         in_specs=[pl.BlockSpec(memory_space=pl.ANY)] + [vmem] * 12,
         out_specs=(pl.BlockSpec(memory_space=pl.ANY), vmem, vmem),
         scratch_shapes=[
-            pltpu.VMEM((2, strips, 4, cols_here, width), bf16),
+            pltpu.VMEM((4, strips, 2, cols_here, width), bf16),
             pltpu.VMEM((width // 128, devices, 32, 128), jnp.float32),
             pltpu.VMEM((2, 2, devices, 16, width), bf16),
             pltpu.VMEM((2, 2, devices, 16, width), bf16),
-            pltpu.VMEM((4 * length, width // 128, 128), jnp.float32),
+            pltpu.VMEM((width // 128, 4 * length, 128), jnp.float32),
             pltpu.VMEM((8, bands, length // bands, width), bf16),
             pltpu.VMEM((8, bands, length // bands, width), bf16),
             pltpu.VMEM((8, devices * 8, length), bf16),
@@ -484,8 +523,8 @@
             pltpu.VMEM((devices, 1, 128), jnp.float32),
             pltpu.VMEM((devices, 1, 128), jnp.float32),
             pltpu.VMEM((devices, 1, 128), jnp.float32),
-            pltpu.SemaphoreType.DMA((2,)),
-            pltpu.SemaphoreType.DMA((2,)),
+            pltpu.SemaphoreType.DMA((4,)),
+            pltpu.SemaphoreType.DMA((4,)),
             pltpu.SemaphoreType.DMA((2, 2)),
             pltpu.SemaphoreType.DMA((2, 2)),
             pltpu.SemaphoreType.DMA((8,)),
@@ -516,11 +555,7 @@
         decode_first,
         decode_second,
     )
-    final_field = (
-        final.reshape(2, 4, bands, rows_here, width)
-        .transpose(3, 2, 1, 0, 4)
-        .reshape(rows_here, cols_here, width)
-    )
+    final_field = assemble(final)
     return (final_field, power[0], fleet[0, 0])
 
 

time: 147 us -> 147 us (level)
  Pallas kernels: 138 us -> 144 us
  local copies, waits for them, and re-layouts: 6.48 us -> 0.52 us
    pallas_call x0 -> x1, Pallas kernels: none -> 6.03 us  [assemble(): pl.pallas_call(assemble_kernel, grid=(rows // step,), out_shape=jax.Shape...]
    transpose x1 -> x0, local copies, waits for them, and re-layouts: 3.75 us -> none  [fast_body(): final_field = final.reshape(2, 4, bands, rows_here, width).transpose(3, 2...]
    reshape x1 -> x0, local copies, waits for them, and re-layouts: 2.21 us -> none  [fast_body(): final_field = final.reshape(2, 4, bands, rows_here, width).transpose(3, 2...]
where the time goes in v2:
time: 147 us
  Pallas kernels  144 us (98%)
  between operations  1.83 us (1%)
    pallas_call x1, Pallas kernels, fast_body(): pl.pallas_call(whole_kernel, out_shape=(jax.ShapeDtypeStruct((8, bands, r...  138 us
    pallas_call x1, Pallas kernels, assemble(): pl.pallas_call(assemble_kernel, grid=(rows // step,), out_shape=jax.Shape...  6.03 us

profile of v2, /device:TPU:0, one launch (start us, length us, event | category | flops | bytes accessed | tf_op | source)
XLA Modules:
  0.0 147.0 jit_solution(1687854354761258092)
XLA Ops:
  0.6 0.8 compare_convert_fusion.head_sum
  1.4 137.9 %shard_map.139 = (bf16[8,4,64,512]{3,2,1,0:T(8,128)(2,1)}, f32[1,128]{1,0:T(1,128)}, f32[1,128]{1,0:T(1,128)}) custom-call(bf16[64,32,512]{2,1,0:T(8,128)(2,1)} %cloud.1, f32[1,512]{1,0:T(1,128)} %bitcast.8, bf16[512,1536]{1,0:T(8,128)(2,1)} %row_qkv.1, bf16[512,512]{1,0:T(8,128)(2,1)} %row_out.1, f32[1,512]{1,0:T(1,128)} %bitcast.9, ...), custom_call_target="tpu_custom_call" | custom-call | flops 10737418240 | bytes 8388608 | tf_op jit(solution)/shard_map/pallas_call | solution.py:502
  139.3 0.0 copy-start.1
  139.3 0.0 copy-start
  139.3 6.0 %shard_map.140 = bf16[64,32,512]{2,1,0:T(8,128)(2,1)} custom-call(bf16[8,4,64,512]{3,2,1,0:T(8,128)(2,1)} %get-tuple-element.6.blocks), custom_call_target="tpu_custom_call" | custom-call | bytes 4194304 | tf_op jit(solution)/shard_map/pallas_call | solution.py:465
  145.3 0.0 copy-done.1
  145.3 0.5 copy.17
  145.9 0.0 copy-done
  (1 shorter events, 0.0 us)
Async XLA Ops:
  139.3 6.1 %copy-start.1 = (f32[1,128]{1,0:T(1,128)S(1)}, f32[1,128]{1,0:T(1,128)}, u32[]{:S(2)}) copy-start(f32[1,128]{1,0:T(1,128)} %get-tuple-element.7) | copy-start | bytes 1540
  139.3 6.6 %copy-start = (f32[1,128]{1,0:T(1,128)S(1)}, f32[1,128]{1,0:T(1,128)}, u32[]{:S(2)}) copy-start(f32[1,128]{1,0:T(1,128)} %get-tuple-element.8) | copy-start | bytes 1540

commit v3 on v2

--- a/solution.py
+++ b/solution.py
@@ -144,21 +144,16 @@
     return x + jnp.dot(context, weight_out[...], preferred_element_type=jnp.float32)
 
 
-def head_sum_matrix(width):
-    head = width // HEADS
-    index = jnp.arange(4 * head, dtype=jnp.int32) // head
-    return (index[:, None] == index[None, :]).astype(jnp.bfloat16)
-
-
 MESH = pl.DeviceIdType.MESH
 
 def whole_kernel(
-    cloud, row_gain, row_qkv, row_out, col_gain, col_qkv, col_out, head_sum,
-    cells, owners, capacity, first, second,
+    cloud, row_gain, col_gain, cells, owners, capacity, second,
+    row_qkv_in, row_out_in, col_qkv_in, col_out_in, first_in,
     final, power, fleet,
     rows_in, mixed, rows_out, cols_in, columns, cols_out, blocks_in, picks,
     sites_out, sites_in, listed_out, listed_in, yields_out, returned,
-    rows_sent, rows_got, turn_sent, turn_got, cols_sent, cols_got, site_sems, done_sems,
+    field, placed, row_qkv, row_out, col_qkv, col_out, first, head_sum,
+    rows_sent, rows_got, turn_sent, turn_got, cols_sent, cols_got, site_sems, done_sem, weight_sems,
 ):
     strips = lax.axis_size("strip")
     bands = lax.axis_size("band")
@@ -175,6 +170,18 @@
     def split(number):
         return (number // strips, number % strips)
 
+    weights = [
+        pltpu.make_async_copy(source, target, weight_sems.at[number])
+        for number, (source, target) in enumerate(
+            (
+                (row_qkv_in, row_qkv),
+                (row_out_in, row_out),
+                (col_qkv_in, col_qkv),
+                (col_out_in, col_out),
+                (first_in, first),
+            )
+        )
+    ]
     barrier = pltpu.get_barrier_semaphore()
 
     @pl.loop(1, devices)
@@ -203,6 +210,16 @@
             cloud.at[pl.ds(strip * 8 + part * 2, 2)], rows_in.at[part, strip], rows_got.at[part]
         ).start()
 
+    for copy in weights:
+        copy.start()
+    head = width // HEADS
+    head_sum[...] = jnp.where(
+        lax.broadcasted_iota(jnp.int32, head_sum.shape, 0) // head
+        == lax.broadcasted_iota(jnp.int32, head_sum.shape, 1) // head,
+        1.0,
+        0.0,
+    ).astype(jnp.bfloat16)
+
     plants = cells.shape[1]
     slots = 8
     owner_hot = lax.broadcasted_iota(jnp.int32, (devices, plants), 0) == owners[...]
@@ -267,6 +284,31 @@
             preferred_element_type=jnp.float32,
         ).astype(jnp.bfloat16)
 
+    def send_turn(parity, part):
+        @pl.loop(1, devices)
+        def _(step):
+            to_band, to_strip = split((me + step) % devices)
+            pltpu.make_async_remote_copy(
+                src_ref=rows_out.at[part, parity, to_strip * bands + to_band],
+                dst_ref=cols_in.at[parity, part, me],
+                send_sem=turn_sent.at[parity, part],
+                recv_sem=turn_got.at[parity, part],
+                device_id=(to_band, to_strip),
+                device_id_type=MESH,
+            ).start()
+
+        pltpu.make_async_copy(
+            rows_out.at[part, parity, strip * bands + band],
+            cols_in.at[parity, part, me],
+            turn_got.at[parity, part],
+        ).start()
+
+    def turn_left(parity, part):
+        wait_bytes(cols_in.at[parity, part, pl.ds(0, devices - 1)], turn_sent.at[parity, part])
+
+    weights[0].wait()
+    weights[1].wait()
+
     @pl.loop(0, 2)
     def _(part):
         @pl.loop(0, 4)
@@ -293,23 +335,13 @@
                     taken.astype(jnp.bfloat16).reshape(devices, 16, 128)
                 )
 
-            @pl.loop(1, devices)
-            def _(step):
-                to_band, to_strip = split((me + step) % devices)
-                pltpu.make_async_remote_copy(
-                    src_ref=rows_out.at[part, parity, to_strip * bands + to_band],
-                    dst_ref=cols_in.at[parity, part, me],
-                    send_sem=turn_sent.at[parity, part],
-                    recv_sem=turn_got.at[parity, part],
-                    device_id=(to_band, to_strip),
-                    device_id_type=MESH,
-                ).start()
-
-            pltpu.make_async_copy(
-                rows_out.at[part, parity, strip * bands + band],
-                cols_in.at[parity, part, me],
-                turn_got.at[parity, part],
-            ).start()
+        send_turn(0, part)
+
+    for part in range(2):
+        turn_left(0, part)
+        send_turn(1, part)
+    weights[2].wait()
+    weights[3].wait()
 
     @pl.loop(0, 2)
     def _(parity):
@@ -356,12 +388,17 @@
     sites = jnp.zeros((devices * slots, width), jnp.float32)
     for col in range(8):
         wait_bytes(blocks_in.at[col], cols_got.at[col])
-        pltpu.make_async_copy(blocks_in.at[col], final.at[col], done_sems.at[col]).start()
         sites = sites + jnp.dot(
             picks[col],
             blocks_in[col].reshape(length, width),
             preferred_element_type=jnp.float32,
         )
+        for src in range(4):
+            at = src * 8 + 2 * (col % 4) + col // 4
+            for lanes in range(0, width, 128):
+                field[lanes // 128, pl.ds(at, rows_here, stride=cols_here), :] = blocks_in[
+                    col, src, :, lanes : lanes + 128
+                ].astype(jnp.float32)
     sites = sites.reshape(devices, slots, width)
     half = width // 2
     sites_out[...] = jnp.concatenate([sites[:, :, :half], sites[:, :, half:]], axis=1).astype(
@@ -381,6 +418,17 @@
         ).start()
 
     pltpu.make_async_copy(sites_out.at[me], sites_in.at[me], site_sems.at[1]).start()
+
+    @pl.loop(0, rows_here // 8)
+    def _(row):
+        tokens = pl.ds(pl.multiple_of(row * 8 * cols_here, 256), 8 * cols_here)
+        for lanes in range(0, width, 128):
+            placed[pl.ds(row * 8, 8), :, lanes : lanes + 128] = (
+                field[lanes // 128, tokens, :].astype(jnp.bfloat16).reshape(8, cols_here, 128)
+            )
+
+    pltpu.make_async_copy(placed, final, done_sem).start()
+    weights[4].wait()
     wait_bytes(listed_in, site_sems.at[5])
     wait_bytes(sites_in, site_sems.at[1])
 
@@ -417,13 +465,9 @@
     for pair in range(4):
         wait_bytes(rows_in.at[pair, pl.ds(0, strips - 1)], rows_sent.at[pair])
     for part in range(2):
-        for parity in range(2):
-            wait_bytes(
-                cols_in.at[parity, part, pl.ds(0, devices - 1)], turn_sent.at[parity, part]
-            )
+        turn_left(1, part)
     for col in range(8):
         wait_bytes(cols_out.at[col, pl.ds(0, bands - 1)], cols_sent.at[col])
-        wait_bytes(blocks_in.at[col], done_sems.at[col])
     wait_bytes(sites_out.at[pl.ds(0, devices - 1)], site_sems.at[0])
     wait_bytes(listed_out.at[pl.ds(0, devices - 1)], site_sems.at[4])
 
@@ -441,39 +485,7 @@
     sums = jnp.sum(jnp.where(lane[:, 0] == slots, back, 0.0), axis=(0, 1), keepdims=True)
     fleet[...] = jnp.broadcast_to(sums / float(plants * devices), fleet.shape)
     wait_bytes(yields_out.at[pl.ds(0, devices - 1)], site_sems.at[2])
-
-
-def assemble_kernel(blocks, out, tile):
-    parts, bands, rows, width = blocks.shape
-    cols = parts * bands
-    for lanes in range(0, width, 128):
-        for part in range(parts):
-            for band in range(bands):
-                at = band * parts + 2 * (part % 4) + part // 4
-                tile[lanes // 128, pl.ds(at, rows, stride=cols), :] = blocks[
-                    part, band, :, lanes : lanes + 128
-                ].astype(jnp.float32)
-        out[:, :, lanes : lanes + 128] = (
-            tile[lanes // 128].astype(jnp.bfloat16).reshape(rows, cols, 128)
-        )
-
-
-def assemble(blocks):
-    parts, bands, rows, width = blocks.shape
-    step = 16
-    cols = parts * bands
-    return pl.pallas_call(
-        assemble_kernel,
-        grid=(rows // step,),
-        out_shape=jax.ShapeDtypeStruct((rows, cols, width), blocks.dtype),
-        in_specs=[pl.BlockSpec((parts, bands, step, width), lambda i: (0, 0, i, 0))],
-        out_specs=pl.BlockSpec((step, cols, width), lambda i: (i, 0, 0)),
-        scratch_shapes=[pltpu.VMEM((width // 128, step * cols, 128), jnp.float32)],
-        compiler_params=pltpu.CompilerParams(vmem_limit_bytes=60 * 1024 * 1024),
-        cost_estimate=pl.CostEstimate(
-            flops=0, bytes_accessed=4 * blocks.size, transcendentals=0
-        ),
-    )(blocks)
+    wait_bytes(placed, done_sem)
 
 
 def fast_body(
@@ -498,16 +510,18 @@
     plants_here = plant_cell.shape[0]
 
     vmem = pl.BlockSpec(memory_space=pltpu.VMEM)
+    anywhere = pl.BlockSpec(memory_space=pl.ANY)
+    half = 4 * (width // HEADS)
     bf16 = jnp.bfloat16
-    final, power, fleet = pl.pallas_call(
+    final_field, power, fleet = pl.pallas_call(
         whole_kernel,
         out_shape=(
-            jax.ShapeDtypeStruct((8, bands, rows_here, width), bf16),
+            jax.ShapeDtypeStruct(cloud_field.shape, bf16),
             jax.ShapeDtypeStruct((1, plants_here), jnp.float32),
             jax.ShapeDtypeStruct((1, 128), jnp.float32),
         ),
-        in_specs=[pl.BlockSpec(memory_space=pl.ANY)] + [vmem] * 12,
-        out_specs=(pl.BlockSpec(memory_space=pl.ANY), vmem, vmem),
+        in_specs=[anywhere] + [vmem] * 6 + [anywhere] * 5,
+        out_specs=(anywhere, vmem, vmem),
         scratch_shapes=[
             pltpu.VMEM((4, strips, 2, cols_here, width), bf16),
             pltpu.VMEM((width // 128, devices, 32, 128), jnp.float32),
@@ -523,6 +537,14 @@
             pltpu.VMEM((devices, 1, 128), jnp.float32),
             pltpu.VMEM((devices, 1, 128), jnp.float32),
             pltpu.VMEM((devices, 1, 128), jnp.float32),
+            pltpu.VMEM((width // 128, rows_here * cols_here, 128), jnp.float32),
+            pltpu.VMEM(cloud_field.shape, bf16),
+            pltpu.VMEM(row_qkv.shape, bf16),
+            pltpu.VMEM(row_out.shape, bf16),
+            pltpu.VMEM(col_qkv.shape, bf16),
+            pltpu.VMEM(col_out.shape, bf16),
+            pltpu.VMEM(decode_first.shape, bf16),
+            pltpu.VMEM((half, half), bf16),
             pltpu.SemaphoreType.DMA((4,)),
             pltpu.SemaphoreType.DMA((4,)),
             pltpu.SemaphoreType.DMA((2, 2)),
@@ -530,7 +552,8 @@
             pltpu.SemaphoreType.DMA((8,)),
             pltpu.SemaphoreType.DMA((8,)),
             pltpu.SemaphoreType.DMA((6,)),
-            pltpu.SemaphoreType.DMA((8,)),
+            pltpu.SemaphoreType.DMA,
+            pltpu.SemaphoreType.DMA((5,)),
         ],
         compiler_params=pltpu.CompilerParams(
             collective_id=0, has_side_effects=True, vmem_limit_bytes=56 * 1024 * 1024
@@ -543,19 +566,17 @@
     )(
         cloud_field,
         row_gain.reshape(1, width),
-        row_qkv,
-        row_out,
         col_gain.reshape(1, width),
-        col_qkv,
-        col_out,
-        head_sum_matrix(width),
         plant_cell.reshape(1, plants_here),
         plant_decoder_device.reshape(1, plants_here),
         plant_capacity.reshape(1, plants_here),
+        decode_second,
+        row_qkv,
+        row_out,
+        col_qkv,
+        col_out,
         decode_first,
-        decode_second,
-    )
-    final_field = assemble(final)
+    )
     return (final_field, power[0], fleet[0, 0])
 
 

time: 147 us -> 137 us (0.932)
  Pallas kernels: 144 us -> 131 us
  local copies, waits for them, and re-layouts: 0.52 us -> 3.68 us
    pallas_call x2 -> x1, Pallas kernels: 144 us -> 131 us  [fast_body(): pl.pallas_call(whole_kernel, out_shape=(jax.ShapeDtypeStruct(cloud_field....]
    unnamed x5 -> x6, local copies, waits for them, and re-layouts: 0.52 us -> 3.68 us
where the time goes in v3:
time: 137 us; the launch traced here: 136 us
  Pallas kernels  131 us (96%)
  local copies, waits for them, and re-layouts  3.68 us (3%)
  between operations  1.83 us (1%)
    pallas_call x1, Pallas kernels, fast_body(): pl.pallas_call(whole_kernel, out_shape=(jax.ShapeDtypeStruct(cloud_field....  131 us
    unnamed x6, local copies, waits for them, and re-layouts  3.68 us

profile of v3, /device:TPU:0, one launch (start us, length us, event | category | flops | bytes accessed | tf_op | source)
XLA Modules:
  0.0 136.4 jit_solution(2545028775501660783)
XLA Ops:
  0.6 130.9 %shard_map.139 = (bf16[64,32,512]{2,1,0:T(8,128)(2,1)}, f32[1,128]{1,0:T(1,128)}, f32[1,128]{1,0:T(1,128)}) custom-call(bf16[64,32,512]{2,1,0:T(8,128)(2,1)} %cloud.1, f32[1,512]{1,0:T(1,128)} %bitcast.8, f32[1,512]{1,0:T(1,128)} %bitcast.9, s32[1,128]{1,0:T(1,128)} %bitcast.10, s32[1,128]{1,0:T(1,128)} %bitcast.11, s32[1,128]{1,0:T(1,128)} %bitcast.12, ...), custom_call_target="tpu_custom_call" | custom-call | flops 10737418240 | bytes 8388608 | tf_op jit(solution)/shard_map/pallas_call | solution.py:516
  131.5 0.0 copy-start.1
  131.5 0.0 copy-start
  131.6 3.2 %copy.18 = bf16[64,32,512]{2,1,0:T(8,128)(2,1)} copy(bf16[64,32,512]{2,1,0:T(8,128)(2,1)} %get-tuple-element.12) | data formatting | bytes 4194304
  134.7 0.0 copy-done.1
  134.7 0.5 copy.19
  135.2 0.0 copy-done
Async XLA Ops:
  131.5 3.2 %copy-start.1 = (f32[1,128]{1,0:T(1,128)S(1)}, f32[1,128]{1,0:T(1,128)}, u32[]{:S(2)}) copy-start(f32[1,128]{1,0:T(1,128)} %get-tuple-element.7) | copy-start | bytes 1540
  131.5 3.7 %copy-start = (f32[1,128]{1,0:T(1,128)S(1)}, f32[1,128]{1,0:T(1,128)}, u32[]{:S(2)}) copy-start(f32[1,128]{1,0:T(1,128)} %get-tuple-element.8) | copy-start | bytes 1540

commit v4 on v3

--- a/solution.py
+++ b/solution.py
@@ -192,8 +192,7 @@
 
     pl.semaphore_wait(barrier, devices - 1)
 
-    @pl.loop(0, 4)
-    def _(part):
+    def send_rows(part):
         @pl.loop(1, strips)
         def _(step):
             to = (strip + step) % strips
@@ -210,6 +209,8 @@
             cloud.at[pl.ds(strip * 8 + part * 2, 2)], rows_in.at[part, strip], rows_got.at[part]
         ).start()
 
+    send_rows(0)
+    send_rows(1)
     for copy in weights:
         copy.start()
     head = width // HEADS
@@ -315,6 +316,11 @@
         def _(row):
             pair = part * 2 + row // 2
 
+            @pl.when((row % 2 == 0) & (part == 0))
+            def _():
+                wait_bytes(rows_in.at[pair, pl.ds(0, strips - 1)], rows_sent.at[pair])
+                send_rows(pair + 2)
+
             @pl.when(row % 2 == 0)
             def _():
                 wait_bytes(rows_in.at[pair], rows_got.at[pair])
@@ -462,7 +468,7 @@
 
     pltpu.make_async_copy(yields_out.at[me], returned.at[me], site_sems.at[3]).start()
 
-    for pair in range(4):
+    for pair in range(2, 4):
         wait_bytes(rows_in.at[pair, pl.ds(0, strips - 1)], rows_sent.at[pair])
     for part in range(2):
         turn_left(1, part)

time: 137 us -> 137 us (level)
  no operation moved by 1% of the time
where the time goes in v4:
time: 137 us
  Pallas kernels  131 us (96%)
  local copies, waits for them, and re-layouts  3.68 us (3%)
  between operations  1.83 us (1%)
    pallas_call x1, Pallas kernels, fast_body(): pl.pallas_call(whole_kernel, out_shape=(jax.ShapeDtypeStruct(cloud_field....  131 us
    unnamed x6, local copies, waits for them, and re-layouts  3.68 us

profile of v4, /device:TPU:0, one launch (start us, length us, event | category | flops | bytes accessed | tf_op | source)
XLA Modules:
  0.0 136.5 jit_solution(17434603862050797369)
XLA Ops:
  0.6 131.0 %shard_map.139 = (bf16[64,32,512]{2,1,0:T(8,128)(2,1)}, f32[1,128]{1,0:T(1,128)}, f32[1,128]{1,0:T(1,128)}) custom-call(bf16[64,32,512]{2,1,0:T(8,128)(2,1)} %cloud.1, f32[1,512]{1,0:T(1,128)} %bitcast.8, f32[1,512]{1,0:T(1,128)} %bitcast.9, s32[1,128]{1,0:T(1,128)} %bitcast.10, s32[1,128]{1,0:T(1,128)} %bitcast.11, s32[1,128]{1,0:T(1,128)} %bitcast.12, ...), custom_call_target="tpu_custom_call" | custom-call | flops 10737418240 | bytes 8388608 | tf_op jit(solution)/shard_map/pallas_call | solution.py:522
  131.7 0.0 copy-start.1
  131.7 0.0 copy-start
  131.7 3.2 %copy.18 = bf16[64,32,512]{2,1,0:T(8,128)(2,1)} copy(bf16[64,32,512]{2,1,0:T(8,128)(2,1)} %get-tuple-element.12) | data formatting | bytes 4194304
  134.8 0.0 copy-done.1
  134.8 0.5 copy.19
  135.3 0.0 copy-done
Async XLA Ops:
  131.7 3.2 %copy-start.1 = (f32[1,128]{1,0:T(1,128)S(1)}, f32[1,128]{1,0:T(1,128)}, u32[]{:S(2)}) copy-start(f32[1,128]{1,0:T(1,128)} %get-tuple-element.7) | copy-start | bytes 1540
  131.7 3.7 %copy-start = (f32[1,128]{1,0:T(1,128)S(1)}, f32[1,128]{1,0:T(1,128)}, u32[]{:S(2)}) copy-start(f32[1,128]{1,0:T(1,128)} %get-tuple-element.8) | copy-start | bytes 1540
